TPU v7x, 32 devices: a whole 2x2x4 slice. The times are simulated.
32 devices in a mesh: comp: 8 (over z, core), feat: 4 (over y, x).
Axes of the slice: x: 2, y: 2, z: 4, core: 2. Of those that a mesh axis runs over, the one named last changes fastest.
Arguments:
- block_values: bfloat16 [8, 4, 24, 128, 128], P('comp', 'feat'), may hold values from -0.125 to 0.125
- block_rows: int32 [8, 4, 24], P('comp', 'feat'), may hold values from 0 to 15, as said below
- block_cols: int32 [8, 4, 24], P('comp', 'feat'), may hold values from 0 to 13, as said below
- block_counts: int32 [8, 4], P('comp', 'feat'), may hold values from 8 to 24, as said below
- right_side: float32 [16384, 128], P(('comp', 'feat')), may hold values from -6 to 6
- ridge: float32 [128], replicated, may hold values from 0.1 to 2
Outputs:
- solution: float32 [7168, 128], P('feat')
- residual: float32 [16384, 128], P(('comp', 'feat'))
Inputs may be any that keep to these rules, and one draw needn't show every extreme that they name: Within one device the listed (block_rows, block_cols) pairs of all 24 slots are distinct; block rows are very uneven in how many blocks they hold. `block_cols`: see block_rows. `block_counts`: slots at or beyond a device's count are ignored; some device is full in every draw.
All inputs are finite; a program needn't handle non-finite values.
Results may differ from a plain program's by a relative error of at most 0.0029.
Values may be sent and summed in bfloat16 or wider, within the bound.
A program may use at most 64 MiB of HBM per device.

v0:
```python
import jax
import jax.numpy as jnp
from jax import lax
from jax.sharding import PartitionSpec as P

RB_DEV = 16
CB_DEV = 14
ITERS = 2


def shards(block_values, block_rows, block_cols, block_counts, right_side, ridge):
    values = block_values[0, 0]
    slot_rows = block_rows[0, 0]
    slot_cols = block_cols[0, 0]
    count_of_slots = block_counts[0, 0]
    responses = right_side.shape[1]
    total_slot_number = values.shape[0]
    block_edge = values.shape[1]
    slot_live = (jnp.arange(total_slot_number) < count_of_slots).astype(jnp.float32)
    row_lookup_table = (jnp.arange(RB_DEV)[:, None] == slot_rows[None, :]).astype(
        jnp.float32
    ) * slot_live[None, :]
    col_table = (jnp.arange(CB_DEV)[:, None] == slot_cols[None, :]).astype(jnp.float32) * slot_live[
        None, :
    ]
    first_comp = (lax.axis_index("comp") == 0).astype(jnp.float32)

    def backward(low_slab):
        row_slabs = low_slab.reshape(RB_DEV, block_edge, responses)
        selected = jnp.take(row_slabs, slot_rows, axis=0)
        block_products = jnp.einsum(
            "sij,sik->sjk", values, selected, preferred_element_type=jnp.float32
        )
        summed = jnp.einsum(
            "qs,sjk->qjk", col_table, block_products, precision=lax.Precision.HIGHEST
        )
        return summed.reshape(CB_DEV * block_edge, responses)

    residual = right_side
    image_weight = 1.0

    def slab_of(current):
        return lax.all_gather(current.astype(jnp.bfloat16), "feat", axis=0, tiled=True)

    def reduce_grad(partial_contribution):
        return lax.psum(partial_contribution, "comp")

    def grad_total(gradient):
        return lax.psum(first_comp * jnp.sum(gradient * gradient, axis=0), ("comp", "feat"))

    gradient = reduce_grad(backward(slab_of(residual)))
    energy = grad_total(gradient)
    search_direction = gradient
    solution = jnp.zeros_like(gradient)
    for step_index in range(ITERS):
        col_panels = search_direction.astype(jnp.bfloat16).reshape(CB_DEV, block_edge, responses)
        forward_selected = jnp.take(col_panels, slot_cols, axis=0)
        forward_block_products = jnp.einsum(
            "sij,sjk->sik", values, forward_selected, preferred_element_type=jnp.float32
        )
        forward_summed = jnp.einsum(
            "rs,sik->rik", row_lookup_table, forward_block_products, precision=lax.Precision.HIGHEST
        )
        image_rows = lax.psum_scatter(
            forward_summed.reshape(RB_DEV * block_edge, responses),
            "feat",
            scatter_dimension=0,
            tiled=True,
        )
        image_energy, direction_energy = lax.psum(
            (
                image_weight * jnp.sum(image_rows * image_rows, axis=0),
                first_comp * jnp.sum(search_direction * search_direction, axis=0),
            ),
            ("comp", "feat"),
        )
        step_size = energy / (image_energy + ridge * direction_energy)
        solution = solution + step_size * search_direction
        residual = residual - step_size * image_rows
        if step_index + 1 < ITERS:
            gradient = reduce_grad(backward(slab_of(residual))) - ridge * solution
            next_energy = grad_total(gradient)
            search_direction = gradient + next_energy / energy * search_direction
            energy = next_energy
    return (solution, residual)


def solution(mesh):
    placed = (
        P("comp", "feat", None, None, None),
        P("comp", "feat", None),
        P("comp", "feat", None),
        P("comp", "feat"),
        P(("comp", "feat"), None),
        P(),
    )
    return jax.shard_map(
        shards,
        mesh=mesh,
        in_specs=placed,
        out_specs=(P("feat", None), P(("comp", "feat"), None)),
        check_vma=False,
    )
```

profile of v0, /device:TPU:0, one launch (start us, length us, event | category | flops | bytes accessed | tf_op | source)
XLA Modules:
  0.0 368.0 jit_solution(12104825385859967408)
XLA Ops:
  10.3 11.5 %all_gather.6 = bf16[2048,128]{1,0:T(8,128)(2,1)S(1)} all-gather(bf16[512,128]{1,0:T(8,128)(2,1)S(1)} %convert_element_type.26), channel_id=1, replica_groups=mesh['comp'=8,'feat'=4] {'feat'}, dimensions={0}, use_global_device_ids=true | all-gather | bytes 655360 | tf_op jit(solution)/shard_map/all_gather | solution.py:43
  22.5 1.7 fusion.14
  24.1 2.0 copy.12
  26.1 1.0 fusion.6
  27.1 1.2 copy.8
  28.5 58.3 %all-reduce.5.cloned.1.call-done = f32[1792,128]{1,0:T(8,128)} async-done(((f32[1792,128]{1,0:T(8,128)}), f32[1792,128]{1,0:T(8,128)}) %all-reduce.5.cloned.1.call-update) | async-done | bytes 917520 | tf_op jit(solution)/shard_map/psum | solution.py:46
  86.8 1.7 multiply_reduce_fusion.2
  89.2 2.0 fusion.12
  91.2 2.0 copy.13
  93.2 1.0 fusion.4
  94.3 1.3 copy.9
  95.7 26.7 %reduce-scatter.3.cloned.1.call-done = f32[512,128]{1,0:T(8,128)} async-done(((f32[2048,128]{1,0:T(8,128)}), f32[512,128]{1,0:T(8,128)}) %reduce-scatter.3.cloned.1.call-update) | async-done | bytes 262160 | tf_op jit(solution)/shard_map/reduce_scatter | solution.py:64
  122.4 1.0 multiply_reduce_fusion.4
  123.4 39.4 %all-reduce.1 = (f32[128]{0:T(128)S(1)}, f32[128]{0:T(128)S(1)}) all-reduce(f32[128]{0:T(128)S(1)} %broadcast_multiply_fusion.2, f32[128]{0:T(128)S(1)} %multiply_reduce_fusion.4), channel_id=1, replica_groups=mesh['comp'=8,'feat'=4] {'comp','feat'}, use_global_device_ids=true, to_apply=%region_2.4 | all-reduce | flops 256 | bytes 2048 | tf_op jit(solution)/shard_map/psum | solution.py:49
  162.8 1.0 fusion.28
  163.8 11.5 %all_gather.7 = bf16[2048,128]{1,0:T(8,128)(2,1)S(1)} all-gather(bf16[512,128]{1,0:T(8,128)(2,1)S(1)} %fusion.28), channel_id=1, replica_groups=mesh['comp'=8,'feat'=4] {'feat'}, dimensions={0}, use_global_device_ids=true | all-gather | bytes 655360 | tf_op jit(solution)/shard_map/all_gather | solution.py:43
  176.0 1.7 fusion.10
  177.7 2.0 copy.14
  179.6 1.0 fusion.2
  180.7 1.2 copy.10
  181.9 57.1 %all-reduce.7.cloned.1.call-done = f32[1792,128]{1,0:T(8,128)} async-done(((f32[1792,128]{1,0:T(8,128)}), f32[1792,128]{1,0:T(8,128)}) %all-reduce.7.cloned.1.call-update) | async-done | bytes 917520 | tf_op jit(solution)/shard_map/psum | solution.py:46
  239.1 1.5 multiply_reduce_fusion.1
  240.6 39.5 %psum.56 = f32[128]{0:T(128)S(1)} all-reduce(f32[128]{0:T(128)S(1)} %broadcast_multiply_fusion.1), channel_id=1, replica_groups=mesh['comp'=8,'feat'=4] {'comp','feat'}, use_global_device_ids=true, to_apply=%region_8.11 | all-reduce | flops 128 | bytes 1024 | tf_op jit(solution)/shard_map/psum | solution.py:49
  280.3 1.6 gather_fusion.3
  281.9 3.1 fusion.8
  285.0 3.0 copy.15
  288.0 2.4 fusion
  290.5 1.3 copy.11
  291.8 27.4 %reduce-scatter.5.cloned.1.call-done = f32[512,128]{1,0:T(8,128)} async-done(((f32[2048,128]{1,0:T(8,128)}), f32[512,128]{1,0:T(8,128)}) %reduce-scatter.5.cloned.1.call-update) | async-done | bytes 262160 | tf_op jit(solution)/shard_map/reduce_scatter | solution.py:64
  319.2 1.0 multiply_reduce_fusion.3
  320.2 39.4 %all-reduce = (f32[128]{0:T(128)S(1)}, f32[128]{0:T(128)S(1)}) all-reduce(f32[128]{0:T(128)S(1)} %multiply_reduce_fusion.3, f32[128]{0:T(128)S(1)} %broadcast_multiply_fusion), channel_id=1, replica_groups=mesh['comp'=8,'feat'=4] {'comp','feat'}, use_global_device_ids=true, to_apply=%region_11.14 | all-reduce | flops 256 | bytes 2048 | tf_op jit(solution)/shard_map/psum | solution.py:70
  359.6 1.1 multiply_add_fusion
  (45 shorter events, 5.8 us)
Async XLA Ops:
  7.2 15.3 %copy-start = (bf16[1,1,24,128,128]{4,3,2,1,0:T(8,128)(2,1)S(1)}, bf16[1,1,24,128,128]{4,3,2,1,0:T(8,128)(2,1)}, u32[]{:S(2)}) copy-start(bf16[1,1,24,128,128]{4,3,2,1,0:T(8,128)(2,1)} %param.10) | copy-start | bytes 2359300
  7.2 79.6 %all-reduce.5.cloned.1.call-start = ((), (), s32[]{:S(2)}) async-start(), calls=%async_computation.2 | async-start | bytes 1835008 | tf_op jit(solution)/shard_map/psum | solution.py:46
  24.1 2.0 copy-start.7
  28.4 94.0 %reduce-scatter.3.cloned.1.call-start = ((), (), s32[]{:S(2)}) async-start(), calls=%async_computation.3 | async-start | bytes 1310720 | tf_op jit(solution)/shard_map/reduce_scatter | solution.py:64
  91.2 2.0 copy-start.8
  94.2 68.6 %copy-start.6 = (f32[128]{0:T(128)S(1)}, f32[128]{0:T(128)}, u32[]{:S(2)}) copy-start(f32[128]{0:T(128)} %param.15) | copy-start | bytes 1540
  94.2 68.6 %copy-start.3 = (f32[512,128]{1,0:T(8,128)S(1)}, f32[512,128]{1,0:T(8,128)}, u32[]{:S(2)}) copy-start(f32[512,128]{1,0:T(8,128)} %param.14) | copy-start | bytes 786436
  95.6 143.5 %all-reduce.7.cloned.1.call-start = ((), (), s32[]{:S(2)}) async-start(), calls=%async_computation.4 | async-start | bytes 1835008 | tf_op jit(solution)/shard_map/psum | solution.py:46
  180.7 58.4 %copy-start.1 = (f32[1792,128]{1,0:T(8,128)S(1)}, f32[1792,128]{1,0:T(8,128)}, u32[]{:S(2)}) copy-start(f32[1792,128]{1,0:T(8,128)} %all-reduce.5.cloned.1.call-done) | copy-start | bytes 2752516
  181.9 137.3 %reduce-scatter.5.cloned.1.call-start = ((), (), s32[]{:S(2)}) async-start(), calls=%async_computation.5 | async-start | bytes 1310720 | tf_op jit(solution)/shard_map/reduce_scatter | solution.py:64
  239.1 41.0 %copy-start.2 = (f32[1792,128]{1,0:T(8,128)S(1)}, f32[1792,128]{1,0:T(8,128)}, u32[]{:S(2)}) copy-start(f32[1792,128]{1,0:T(8,128)} %all-reduce.7.cloned.1.call-done) | copy-start | bytes 2752516
  291.8 69.0 %copy-start.4 = (f32[512,128]{1,0:T(8,128)S(1)}, f32[512,128]{1,0:T(8,128)}, u32[]{:S(2)}) copy-start(f32[512,128]{1,0:T(8,128)} %reduce-scatter.3.cloned.1.call-done) | copy-start | bytes 786436
  359.6 1.2 copy-start.5
Sparse Core Ops, SparseCore 0:
  28.5 58.2 all-reduce.4
  95.7 26.6 reduce-scatter.2
  182.0 56.9 all-reduce.6
  291.9 27.2 reduce-scatter.4
where the time goes:
time: 369 us; the launch traced here: 368 us
  waiting for transfers between devices  170 us (46%)
  blocking collectives  141 us (38%)
  local copies, waits for them, and re-layouts  17.6 us (5%)
  between operations  14.6 us (4%)
  matrix products  13.9 us (4%)
  other arithmetic  10.8 us (3%)
    psum x2, waiting for transfers between devices, reduce_grad(): return lax.psum(partial_contribution, 'comp')  115 us
    psum x2, blocking collectives, grad_total(): lax.psum(first_comp * jnp.sum(gradient * gradient, axis=0), ('comp', 'fea...  78.8 us
    reduce_scatter x2, waiting for transfers between devices, shards(): lax.psum_scatter(forward_summed.reshape(RB_DEV * block_edge, responses),...  54.1 us
    psum x1, blocking collectives, shards(): lax.psum((image_weight * jnp.sum(image_rows * image_rows, axis=0), first_...  39.4 us
    all_gather x2, blocking collectives, slab_of(): lax.all_gather(current.astype(jnp.bfloat16), 'feat', axis=0, tiled=True)  23 us
  transfers between devices with their start and end apart: 4, of which 4 were waited for; matrix products, arithmetic and copies ran while one was open for 0% of the time, Pallas kernels for 0%

commit v1 on v0

v1 whole, which is shorter than its diff:
```python
import functools

import jax
import jax.numpy as jnp
from jax import lax
from jax.experimental import pallas as pl
from jax.experimental.pallas import tpu as pltpu
from jax.sharding import PartitionSpec as P

CB_DEV = 14
MESH = pl.DeviceIdType.MESH
F32 = jnp.float32
BF16 = jnp.bfloat16


def kernel(
    nz, nf, slots, rb, edge, sr,
    rows, cols, count, values, rs, ridge, sol_out, res_out,
    vt, run, slab_a, slab_b, part, sib, pair, zbuf, dirs, panels, img, rbuf, g_f32, i_f32,
    link, sc_src, sc_feat, sc_mid, sc_comp, send_sems, recv_sems,
):
    comp, feat = lax.axis_index("comp"), lax.axis_index("feat")
    core, z = lax.rem(comp, 2), comp // 2
    half = CB_DEV // 2 * edge
    hp = nz * sr
    own_blocks = rb // nf
    sibling = {"comp": comp + 1 - 2 * core}
    n_comp = 2 * nz
    pending = []
    used = [0]

    def zpeer(k):
        return {"comp": lax.rem(z + k, nz) * 2 + core}

    def fpeer(k):
        return {"feat": lax.rem(feat + k, nf)}

    def cpeer(k):
        return {"comp": lax.rem(comp + k, n_comp)}

    def send(src, dst, device):
        at = used[0]
        used[0] += 1
        copy = pltpu.make_async_remote_copy(
            src_ref=src,
            dst_ref=dst,
            send_sem=send_sems.at[at],
            recv_sem=recv_sems.at[at],
            device_id=device,
            device_id_type=MESH,
        )
        copy.start()
        pending.append(copy)
        return copy

    def shard(k):
        return pl.multiple_of(lax.rem(z + k, nz) * sr, 16)

    slabs = (slab_a, slab_b)
    prev_c, last_c = 0, slots
    prev_r, last_r = slots + CB_DEV, 2 * slots + CB_DEV

    def last_slot(keys, wanted, limit):
        found = jnp.int32(slots)
        for t in range(slots):
            found = jnp.where((keys[t] == wanted) & (t < limit), t, found)
        return found

    def make_links(keys, groups, prev, last):
        @pl.loop(0, slots)
        def _(s):
            link[prev + s] = last_slot(keys, keys[s], s)

        live = count[0]

        @pl.loop(0, groups)
        def _(q):
            link[last + q] = last_slot(keys, q, live)

    barrier = pltpu.get_barrier_semaphore()
    for k in range(1, n_comp):
        pl.semaphore_signal(barrier, inc=1, device_id=cpeer(k), device_id_type=MESH)
    for k in range(1, nf):
        pl.semaphore_signal(barrier, inc=1, device_id=fpeer(k), device_id_type=MESH)
    mine = pl.ds(feat * own_blocks, own_blocks)
    slab_a[mine] = rs[...].astype(BF16).reshape(own_blocks, edge, edge)
    pl.semaphore_wait(barrier, n_comp - 1 + nf - 1)

    def gather_feat(which):
        return [
            send(slabs[which].at[mine], slabs[which].at[mine], fpeer(k)) for k in range(1, nf)
        ]

    def backward(which):
        for s in range(slots):
            product = jnp.dot(vt[s], slabs[which][rows[s]], preferred_element_type=F32)
            run[s] = product + run[link[prev_c + s]]
        for q in range(CB_DEV):
            h, p = q // (CB_DEV // 2), q % (CB_DEV // 2)
            part[which, pl.ds(h * hp + p * edge, edge)] = run[link[last_c + q]]
        if hp > half:
            for h in range(2):
                part[which, pl.ds(h * hp + half, hp - half)] = jnp.zeros((hp - half, edge), F32)

    def scatter_comp(which):
        order = list(range(1, nz)) + [0]
        halves = {}
        for k in order:
            theirs = pl.multiple_of((1 - core) * hp + shard(k), 16)
            halves[k] = send(
                part.at[which, pl.ds(theirs, sr)], sib.at[which, pl.ds(shard(k), sr)], sibling
            )
        total = None
        arrivals = []
        for k in order:
            halves[k].wait_recv()
            ours = pl.multiple_of(core * hp + shard(k), 16)
            both = part[which, pl.ds(ours, sr)] + sib[which, pl.ds(shard(k), sr)]
            if k:
                pair[which, k] = both.astype(BF16)
                arrivals.append(send(pair.at[which, k], zbuf.at[which, k], zpeer(k)))
            else:
                total = both
        for k, copy in zip(order, arrivals):
            copy.wait_recv()
            total = total + zbuf[which, k].astype(F32)
        return total

    def gather_comp(which, piece):
        here = pl.ds(pl.multiple_of(core * hp + shard(0), 16), sr)
        dirs[which, here] = piece.astype(BF16)
        across = [send(dirs.at[which, here], dirs.at[which, here], zpeer(k)) for k in range(1, nz)]
        beside = [send(dirs.at[which, here], dirs.at[which, here], sibling)]
        for k, copy in zip(range(1, nz), across):
            copy.wait_recv()
            came = pl.ds(pl.multiple_of(core * hp + shard(nz - k), 16), sr)
            beside.append(send(dirs.at[which, came], dirs.at[which, came], sibling))
        for copy in beside:
            copy.wait_recv()

    def forward(which):
        for q in range(CB_DEV):
            h, p = q // (CB_DEV // 2), q % (CB_DEV // 2)
            panels[q] = dirs[which, pl.ds(h * hp + p * edge, edge)]
        for s in range(slots):
            product = jnp.dot(values[s], panels[cols[s]], preferred_element_type=F32)
            run[s] = product + run[link[prev_r + s]]
        for r in range(rb):
            img[which, r] = run[link[last_r + r]].astype(BF16)

    def scatter_feat(which):
        copies = [
            send(
                img.at[which, pl.ds(lax.rem(feat + k, nf) * own_blocks, own_blocks)],
                rbuf.at[which, k],
                fpeer(k),
            )
            for k in range(1, nf)
        ]
        total = img[which, mine].astype(F32)
        for k, copy in zip(range(1, nf), copies):
            copy.wait_recv()
            total = total + rbuf[which, k].astype(F32)
        return total.reshape(own_blocks * edge, edge)

    def column_sum(x):
        return jnp.sum(x, axis=0, keepdims=True)

    def sums_out(which, rows):
        for i, row in enumerate(rows):
            sc_src[which, pl.ds(i, 1)] = row
        return [send(sc_src.at[which], sc_feat.at[which, k], fpeer(k)) for k in range(1, nf)]

    def sums_on(which, copies):
        total = sc_src[which]
        for k, copy in zip(range(1, nf), copies):
            copy.wait_recv()
            total = total + sc_feat[which, k]
        sc_mid[which] = total
        return [send(sc_mid.at[which], sc_comp.at[which, k], cpeer(k)) for k in range(1, n_comp)]

    def sums_in(which, copies):
        total = sc_mid[which]
        for k, copy in zip(range(1, n_comp), copies):
            copy.wait_recv()
            total = total + sc_comp[which, k]
        return total

    sc_src[...] = jnp.zeros_like(sc_src)
    copies = gather_feat(0)
    run[slots] = jnp.zeros((edge, edge), F32)
    for s in range(slots):
        vt[s] = values[s].T
    make_links(cols, CB_DEV, prev_c, last_c)
    make_links(rows, rb, prev_r, last_r)
    for copy in copies:
        copy.wait_recv()
    backward(0)
    g0 = scatter_comp(0)
    g_f32[...] = g0
    gather_comp(0, g0)
    forward(0)
    i0 = scatter_feat(0)
    i_f32[...] = i0
    g0 = g_f32[...]
    sums = sums_out(0, [column_sum(i0 * i0), column_sum(g0 * g0)])
    first = sums_in(0, sums_on(0, sums))
    penalty = ridge[...]
    image0, energy0 = first[0:1], first[1:2]
    step0 = energy0 / (image0 + penalty * energy0)
    i0 = i_f32[...]
    slab_b[mine] = (rs[...] - step0 * i0).astype(BF16).reshape(own_blocks, edge, edge)
    copies = gather_feat(1)
    for copy in copies:
        copy.wait_recv()
    backward(1)
    g1 = scatter_comp(1)
    g0 = g_f32[...]
    g1 = g1 - penalty * (step0 * g0)
    gather_comp(1, g1)
    energy_row, mixed_row = column_sum(g1 * g1), column_sum(g1 * g0)
    forward(1)
    u = scatter_feat(1)
    i0 = i_f32[...]
    sums = sums_out(1, [column_sum(u * u), column_sum(u * i0), energy_row, mixed_row])
    last = sums_in(1, sums_on(1, sums))
    uu, ui, energy1, gg = last[0:1], last[1:2], last[2:3], last[3:4]
    beta = energy1 / energy0
    curvature = (
        uu + beta * (2.0 * ui + beta * image0)
        + penalty * (energy1 + beta * (2.0 * gg + beta * energy0))
    )
    step1 = energy1 / curvature
    weight = step0 + step1 * beta
    res_out[...] = rs[...] - weight * i0 - step1 * u
    for h in range(2):
        take = pl.ds(h * hp, half)
        sol_out[pl.ds(h * half, half)] = weight * dirs[0, take].astype(F32) + step1 * dirs[
            1, take
        ].astype(F32)
    for copy in pending:
        copy.wait_send()


def shards(nz, nf, block_values, block_rows, block_cols, block_counts, right_side, ridge):
    values = block_values[0, 0]
    rows, cols, count = block_rows[0, 0], block_cols[0, 0], block_counts[0]
    slots, edge = values.shape[0], values.shape[1]
    held = right_side.shape[0]
    rb = held * nf // edge
    half = CB_DEV // 2 * edge
    sr = -(-half // (nz * 16)) * 16
    hp = nz * sr
    own = rb // nf
    n_copies = 2 * (2 * (nf - 1) + 2 * (nz - 1) + 2 * nz + (nf - 1) + (2 * nz - 1))
    smem = pl.BlockSpec(memory_space=pltpu.SMEM)
    vmem = pl.BlockSpec(memory_space=pltpu.VMEM)
    return pl.pallas_call(
        functools.partial(kernel, nz, nf, slots, rb, edge, sr),
        out_shape=(
            jax.ShapeDtypeStruct((CB_DEV * edge, edge), F32),
            jax.ShapeDtypeStruct((held, edge), F32),
        ),
        in_specs=[smem, smem, smem, vmem, vmem, vmem],
        out_specs=(vmem, vmem),
        scratch_shapes=[
            pltpu.VMEM((slots, edge, edge), BF16),
            pltpu.VMEM((slots + 1, edge, edge), F32),
            pltpu.VMEM((rb, edge, edge), BF16),
            pltpu.VMEM((rb, edge, edge), BF16),
            pltpu.VMEM((2, 2 * hp, edge), F32),
            pltpu.VMEM((2, hp, edge), F32),
            pltpu.VMEM((2, nz, sr, edge), BF16),
            pltpu.VMEM((2, nz, sr, edge), BF16),
            pltpu.VMEM((2, 2 * hp, edge), BF16),
            pltpu.VMEM((CB_DEV, edge, edge), BF16),
            pltpu.VMEM((2, rb, edge, edge), BF16),
            pltpu.VMEM((2, nf, own, edge, edge), BF16),
            pltpu.VMEM((sr, edge), F32),
            pltpu.VMEM((held, edge), F32),
            pltpu.SMEM((2 * slots + CB_DEV + rb,), jnp.int32),
            pltpu.VMEM((2, 8, edge), F32),
            pltpu.VMEM((2, nf, 8, edge), F32),
            pltpu.VMEM((2, 8, edge), F32),
            pltpu.VMEM((2, 2 * nz, 8, edge), F32),
            pltpu.SemaphoreType.DMA((n_copies,)),
            pltpu.SemaphoreType.DMA((n_copies,)),
        ],
        compiler_params=pltpu.CompilerParams(
            collective_id=0, has_side_effects=True, vmem_limit_bytes=48 * 1024 * 1024
        ),
        cost_estimate=pl.CostEstimate(
            flops=8 * slots * edge**3, bytes_accessed=4 * 1024 * 1024, transcendentals=0
        ),
    )(rows, cols, count, values, right_side, ridge.reshape(1, edge))


def solution(mesh):
    nz, nf = mesh.shape["comp"] // 2, mesh.shape["feat"]
    placed = (
        P("comp", "feat", None, None, None),
        P("comp", "feat", None),
        P("comp", "feat", None),
        P("comp", "feat"),
        P(("comp", "feat"), None),
        P(),
    )
    return jax.shard_map(
        functools.partial(shards, nz, nf),
        mesh=mesh,
        in_specs=placed,
        out_specs=(P("feat", None), P(("comp", "feat"), None)),
        check_vma=False,
    )
```

time: 369 us -> 90.7 us (0.25)
  waiting for transfers between devices: 170 us -> 0 us
  blocking collectives: 141 us -> 0 us
  Pallas kernels: 0 us -> 84.8 us
  matrix products: 13.9 us -> 0 us
  between operations: 14.6 us -> 1.31 us
  local copies, waits for them, and re-layouts: 17.6 us -> 4.37 us
  other arithmetic: 10.8 us -> 0 us
    psum x3 -> x0, blocking collectives: 118 us -> none  [the longest x2 78.8 us: grad_total(): lax.psum(first_comp * jnp.sum(gradient * gradient, axis=0), ('comp', 'fea...]
    psum x2 -> x0, waiting for transfers between devices: 115 us -> none  [reduce_grad(): return lax.psum(partial_contribution, 'comp')]
    pallas_call x0 -> x1, Pallas kernels: none -> 84.8 us  [shards(): pl.pallas_call(functools.partial(kernel, nz, nf, slots, rb, edge, sr), ou...]
    reduce_scatter x2 -> x0, waiting for transfers between devices: 54.1 us -> none  [shards(): lax.psum_scatter(forward_summed.reshape(RB_DEV * block_edge, responses),...]
    all_gather x2 -> x0, blocking collectives: 23 us -> none  [slab_of(): lax.all_gather(current.astype(jnp.bfloat16), 'feat', axis=0, tiled=True)]
    dot_general x8 -> x0, local copies, waits for them, and re-layouts: 13.9 us -> none  [the longest x2 4.99 us: shards(): jnp.einsum('sij,sjk->sik', values, forward_selected, preferred_element_ty...]
    dot_general x8 -> x0, matrix products: 13.9 us -> none  [the longest x2 5.13 us: shards(): jnp.einsum('sij,sjk->sik', values, forward_selected, preferred_element_ty...]
    reduce_sum x5 -> x0, other arithmetic: 5.56 us -> none  [the longest x2 3.24 us: grad_total(): jnp.sum(gradient * gradient, axis=0)]
  transfers between devices with their start and end apart: 4 -> 0, of which waited for: 4 -> 0; matrix products, arithmetic and copies ran while one was open for 0% -> 0% of each run, Pallas kernels for 0% -> 0%
where the time goes in v1:
time: 90.7 us; the launch traced here: 90.5 us
  Pallas kernels  84.8 us (93%)
  local copies, waits for them, and re-layouts  4.37 us (5%)
  between operations  1.31 us (1%)
    pallas_call x1, Pallas kernels, shards(): pl.pallas_call(functools.partial(kernel, nz, nf, slots, rb, edge, sr), ou...  84.8 us
    unnamed x12, local copies, waits for them, and re-layouts  4.37 us

profile of v1, /device:TPU:0, one launch (start us, length us, event | category | flops | bytes accessed | tf_op | source)
XLA Modules:
  0.0 90.5 jit_solution(17610314520909766819)
XLA Ops:
  1.3 0.0 copy-start.2
  1.3 0.0 copy-start.3
  1.3 0.0 copy-start.4
  1.3 0.6 copy-done.2
  1.9 0.0 copy-done.3
  1.9 0.0 copy-done.4
  2.0 0.0 copy-start
  2.0 1.1 %copy-done = bf16[1,1,24,128,128]{4,3,2,1,0:T(8,128)(2,1)S(1)} copy-done((bf16[1,1,24,128,128]{4,3,2,1,0:T(8,128)(2,1)S(1)}, bf16[1,1,24,128,128]{4,3,2,1,0:T(8,128)(2,1)}, u32[]{:S(2)}) %copy-start) | copy-done | bytes 786456
  3.1 0.0 copy-start.1
  3.1 0.9 %copy-done.1 = f32[512,128]{1,0:T(8,128)S(1)} copy-done((f32[512,128]{1,0:T(8,128)S(1)}, f32[512,128]{1,0:T(8,128)}, u32[]{:S(2)}) %copy-start.1) | copy-done | bytes 262168
  4.0 84.8 %shard_map.77 = (f32[1792,128]{1,0:T(8,128)S(1)}, f32[512,128]{1,0:T(8,128)S(1)}) custom-call(s32[24]{0:T(128)S(1)} %bitcast.7, s32[24]{0:T(128)S(1)} %bitcast.8, s32[1]{0:T(128)} %bitcast.5.count, bf16[24,128,128]{2,1,0:T(8,128)(2,1)S(1)} %bitcast.6, f32[512,128]{1,0:T(8,128)S(1)} %copy-done.1, f32[1,128]{1,0:T(1,128)S(1)} %bitcast.9), custom_call_target="tpu_custom_call" | custom-call | flops 402653184 | bytes 4194304 | tf_op jit(solution)/shard_map/pallas_call | solution.py:258
  88.8 0.9 %copy.11 = f32[1792,128]{1,0:T(8,128)} copy(f32[1792,128]{1,0:T(8,128)S(1)} %get-tuple-element.4) | data formatting | bytes 1835008
  89.8 0.7 copy.12
Async XLA Ops:
  1.3 0.7 copy-start.2
  1.3 0.7 copy-start.3
  1.3 0.7 copy-start.4
  2.0 1.1 %copy-start = (bf16[1,1,24,128,128]{4,3,2,1,0:T(8,128)(2,1)S(1)}, bf16[1,1,24,128,128]{4,3,2,1,0:T(8,128)(2,1)}, u32[]{:S(2)}) copy-start(bf16[1,1,24,128,128]{4,3,2,1,0:T(8,128)(2,1)} %param.6) | copy-start | bytes 2359300
  3.1 0.9 %copy-start.1 = (f32[512,128]{1,0:T(8,128)S(1)}, f32[512,128]{1,0:T(8,128)}, u32[]{:S(2)}) copy-start(f32[512,128]{1,0:T(8,128)} %rs.1) | copy-start | bytes 786436

commit v2 on v1

v2 whole, which is shorter than its diff:
```python
import functools

import jax
import jax.numpy as jnp
from jax import lax
from jax.experimental import pallas as pl
from jax.experimental.pallas import tpu as pltpu
from jax.sharding import PartitionSpec as P

CB_DEV = 14
MESH = pl.DeviceIdType.MESH
F32 = jnp.float32
BF16 = jnp.bfloat16


def fold(x):
    return x + pltpu.roll(x, x.shape[1] // 2, axis=1)


def kernel(
    nz, nf, slots, rb, edge, sr,
    rows, cols, count, values, rs, ridge, sol_out, res_out,
    vt, run_a, run_b, wide_a, wide_b, slabs, part, sib, pair, zbuf, dirs, img, rbuf,
    r_f32, g_f32, i_f32, link, sc_src, sc_feat, sc_mid, sc_comp, send_sems, recv_sems,
):
    comp, feat = lax.axis_index("comp"), lax.axis_index("feat")
    core, z = lax.rem(comp, 2), comp // 2
    low = edge // 2
    half = CB_DEV // 2 * low
    hp = nz * sr
    own_blocks = rb // nf
    sibling = {"comp": comp + 1 - 2 * core}
    n_comp = 2 * nz
    pending = []
    used = [0]
    mine = pl.ds(feat * own_blocks, own_blocks)

    def zpeer(k):
        return {"comp": lax.rem(z + k, nz) * 2 + core}

    def fpeer(k):
        return {"feat": lax.rem(feat + k, nf)}

    def cpeer(k):
        return {"comp": lax.rem(comp + k, n_comp)}

    def send(src, dst, device):
        at = used[0]
        used[0] += 1
        copy = pltpu.make_async_remote_copy(
            src_ref=src,
            dst_ref=dst,
            send_sem=send_sems.at[at],
            recv_sem=recv_sems.at[at],
            device_id=device,
            device_id_type=MESH,
        )
        copy.start()
        pending.append(copy)
        return copy

    def shard(k):
        return pl.multiple_of(lax.rem(z + k, nz) * sr, 16)

    prev_c, last_c = 0, slots
    prev_r, last_r = slots + CB_DEV, 2 * slots + CB_DEV

    def last_slot(keys, wanted, limit):
        found = jnp.int32(slots)
        for t in range(slots):
            found = jnp.where((keys[t] == wanted) & (t < limit), t, found)
        return found

    def make_links(keys, groups, prev, last):
        @pl.loop(0, slots)
        def _(s):
            link[prev + s] = last_slot(keys, keys[s], s)

        live = count[0]

        @pl.loop(0, groups)
        def _(q):
            link[last + q] = last_slot(keys, q, live)

    left = lax.broadcasted_iota(jnp.int32, (low, edge), 1) < low

    def swap(x):
        return pltpu.roll(x, low, axis=1)

    def widen(wide, at, packed):
        x = packed.astype(F32)
        y = swap(x)
        zero = jnp.zeros_like(x)
        wide[at, pl.ds(0, low)] = jnp.where(left, x, zero).astype(BF16)
        wide[at, pl.ds(low, low)] = jnp.where(left, y, zero).astype(BF16)
        wide[at, pl.ds(2 * low, low)] = jnp.where(left, zero, y).astype(BF16)
        wide[at, pl.ds(3 * low, low)] = jnp.where(left, zero, x).astype(BF16)

    def unpack(x0, x1):
        return jnp.where(left, x0, swap(x1)), jnp.where(left, swap(x0), x1)

    def column_sum(x):
        return jnp.sum(x, axis=0, keepdims=True)

    def stream(h):
        run = (run_a, run_b)[h]
        wide = (wide_a, wide_b)[h]

        def gather_feat(it):
            at = (it, h, mine)
            return [send(slabs.at[at], slabs.at[at], fpeer(k)) for k in range(1, nf)]

        def products(blocks, places, prev):
            for s in range(slots):
                block = jnp.concatenate([blocks[s, :low], blocks[s, low:]], axis=1)
                product = jnp.dot(block, wide[places[s]], preferred_element_type=F32)
                run[s] = product + run[link[prev + s]]

        def backward(it):
            for r in range(rb):
                widen(wide, r, slabs[it, h, r])
            products(vt, rows, prev_c)
            for q in range(CB_DEV):
                d, p = q // (CB_DEV // 2), q % (CB_DEV // 2)
                part[it, h, pl.ds(d * hp + p * low, low)] = run[link[last_c + q]]
            if hp > half:
                for d in range(2):
                    part[it, h, pl.ds(d * hp + half, hp - half)] = jnp.zeros((hp - half, edge), F32)

        def scatter_comp(it):
            order = list(range(1, nz)) + [0]
            halves = {}
            for k in order:
                theirs = pl.multiple_of((1 - core) * hp + shard(k), 16)
                halves[k] = send(
                    part.at[it, h, pl.ds(theirs, sr)], sib.at[it, h, pl.ds(shard(k), sr)], sibling
                )
            yield
            arrivals = []
            total = None
            for k in order:
                halves[k].wait_recv()
                ours = pl.multiple_of(core * hp + shard(k), 16)
                both = part[it, h, pl.ds(ours, sr)] + sib[it, h, pl.ds(shard(k), sr)]
                if k:
                    pair[it, h, k] = both.astype(BF16)
                    arrivals.append(send(pair.at[it, h, k], zbuf.at[it, h, k], zpeer(k)))
                else:
                    total = both
            yield
            for k, copy in zip(order, arrivals):
                copy.wait_recv()
                total = total + zbuf[it, h, k].astype(F32)
            return total

        def gather_comp(it, piece):
            here = (it, h, pl.ds(pl.multiple_of(core * hp + shard(0), 16), sr))
            dirs[here] = piece.astype(BF16)
            across = [send(dirs.at[here], dirs.at[here], zpeer(k)) for k in range(1, nz)]
            beside = [send(dirs.at[here], dirs.at[here], sibling)]
            yield
            for k, copy in zip(range(1, nz), across):
                copy.wait_recv()
                came = (it, h, pl.ds(pl.multiple_of(core * hp + shard(nz - k), 16), sr))
                beside.append(send(dirs.at[came], dirs.at[came], sibling))
            yield
            for copy in beside:
                copy.wait_recv()

        def forward(it):
            for q in range(CB_DEV):
                d, p = q // (CB_DEV // 2), q % (CB_DEV // 2)
                widen(wide, q, dirs[it, h, pl.ds(d * hp + p * low, low)])
            products(values, cols, prev_r)
            for r in range(rb):
                img[it, h, r] = run[link[last_r + r]].astype(BF16)

        def scatter_feat(it):
            copies = [
                send(
                    img.at[it, h, pl.ds(lax.rem(feat + k, nf) * own_blocks, own_blocks)],
                    rbuf.at[it, h, k],
                    fpeer(k),
                )
                for k in range(1, nf)
            ]
            yield
            total = img[it, h, mine].astype(F32)
            for k, copy in zip(range(1, nf), copies):
                copy.wait_recv()
                total = total + rbuf[it, h, k].astype(F32)
            return total.reshape(own_blocks * low, edge)

        def sums(it, parts):
            for i, row in enumerate(parts):
                sc_src[it, h, pl.ds(i, 1)] = row
            copies = [
                send(sc_src.at[it, h], sc_feat.at[it, h, k], fpeer(k)) for k in range(1, nf)
            ]
            yield
            total = sc_src[it, h]
            for k, copy in zip(range(1, nf), copies):
                copy.wait_recv()
                total = total + sc_feat[it, h, k]
            sc_mid[it, h] = total
            copies = [
                send(sc_mid.at[it, h], sc_comp.at[it, h, k], cpeer(k)) for k in range(1, n_comp)
            ]
            yield
            for k, copy in zip(range(1, n_comp), copies):
                copy.wait_recv()
                total = total + sc_comp[it, h, k]
            return fold(total)

        copies = gather_feat(0)
        yield
        for copy in copies:
            copy.wait_recv()
        backward(0)
        g0 = yield from scatter_comp(0)
        g_f32[h] = g0
        yield from gather_comp(0, g0)
        forward(0)
        i0 = yield from scatter_feat(0)
        i_f32[h] = i0
        g0 = g_f32[h]
        first = yield from sums(0, [column_sum(i0 * i0), column_sum(g0 * g0)])
        penalty = ridge[pl.ds(h, 1)]
        image0, energy0 = first[0:1], first[1:2]
        step0 = energy0 / (image0 + penalty * energy0)
        r1 = r_f32[h] - step0 * i_f32[h]
        slabs[1, h, mine] = r1.astype(BF16).reshape(own_blocks, low, edge)
        copies = gather_feat(1)
        yield
        for copy in copies:
            copy.wait_recv()
        backward(1)
        g1 = yield from scatter_comp(1)
        g0 = g_f32[h]
        g1 = g1 - penalty * (step0 * g0)
        energy_row, mixed_row = column_sum(g1 * g1), column_sum(g1 * g0)
        yield from gather_comp(1, g1)
        forward(1)
        u = yield from scatter_feat(1)
        i0 = i_f32[h]
        last = yield from sums(
            1, [column_sum(u * u), column_sum(u * i0), energy_row, mixed_row]
        )
        uu, ui, energy1, gg = last[0:1], last[1:2], last[2:3], last[3:4]
        beta = energy1 / energy0
        curvature = (
            uu + beta * (2.0 * ui + beta * image0)
            + penalty * (energy1 + beta * (2.0 * gg + beta * energy0))
        )
        step1 = energy1 / curvature
        weight = step0 + step1 * beta
        r_f32[h] = r_f32[h] - weight * i_f32[h] - step1 * u
        return weight, step1

    barrier = pltpu.get_barrier_semaphore()
    for k in range(1, n_comp):
        pl.semaphore_signal(barrier, inc=1, device_id=cpeer(k), device_id_type=MESH)
    for k in range(1, nf):
        pl.semaphore_signal(barrier, inc=1, device_id=fpeer(k), device_id_type=MESH)
    for r in range(own_blocks):
        top, bottom = rs[pl.ds(r * edge, low)], rs[pl.ds(r * edge + low, low)]
        for h, x in enumerate(unpack(top, bottom)):
            r_f32[h, pl.ds(r * low, low)] = x
    for h in range(2):
        slabs[0, h, mine] = r_f32[h].astype(BF16).reshape(own_blocks, low, edge)
    sc_src[...] = jnp.zeros_like(sc_src)
    pl.semaphore_wait(barrier, n_comp - 1 + nf - 1)

    streams = [stream(h) for h in range(2)]
    steps = [None, None]
    for g in streams:
        next(g)
    run_a[slots] = jnp.zeros((low, edge), F32)
    run_b[slots] = jnp.zeros((low, edge), F32)
    for s in range(slots):
        vt[s] = values[s].T
    make_links(cols, CB_DEV, prev_c, last_c)
    make_links(rows, rb, prev_r, last_r)
    while None in steps:
        for h, g in enumerate(streams):
            try:
                next(g)
            except StopIteration as done:
                steps[h] = done.value
    for r in range(own_blocks):
        parts = unpack(r_f32[0, pl.ds(r * low, low)], r_f32[1, pl.ds(r * low, low)])
        for d in range(2):
            res_out[pl.ds(r * edge + d * low, low)] = parts[d]
    for q in range(CB_DEV):
        d, p = q // (CB_DEV // 2), q % (CB_DEV // 2)
        take = pl.ds(d * hp + p * low, low)
        found = [
            steps[h][0] * dirs[0, h, take].astype(F32) + steps[h][1] * dirs[1, h, take].astype(F32)
            for h in range(2)
        ]
        parts = unpack(*found)
        for d in range(2):
            sol_out[pl.ds(q * edge + d * low, low)] = parts[d]
    for copy in pending:
        copy.wait_send()


def shards(nz, nf, block_values, block_rows, block_cols, block_counts, right_side, ridge):
    values = block_values[0, 0]
    rows, cols, count = block_rows[0, 0], block_cols[0, 0], block_counts[0]
    slots, edge = values.shape[0], values.shape[1]
    held = right_side.shape[0]
    rb = held * nf // edge
    low = edge // 2
    sr = -(-(CB_DEV // 2 * low) // (nz * 16)) * 16
    hp = nz * sr
    own = rb // nf
    n_copies = 4 * (2 * (nf - 1) + 2 * (nz - 1) + 2 * nz + (nf - 1) + (2 * nz - 1))
    penalties = jnp.tile(ridge.reshape(2, low), (1, 2))
    smem = pl.BlockSpec(memory_space=pltpu.SMEM)
    vmem = pl.BlockSpec(memory_space=pltpu.VMEM)
    return pl.pallas_call(
        functools.partial(kernel, nz, nf, slots, rb, edge, sr),
        out_shape=(
            jax.ShapeDtypeStruct((CB_DEV * edge, edge), F32),
            jax.ShapeDtypeStruct((held, edge), F32),
        ),
        in_specs=[smem, smem, smem, vmem, vmem, vmem],
        out_specs=(vmem, vmem),
        scratch_shapes=[
            pltpu.VMEM((slots, edge, edge), BF16),
            pltpu.VMEM((slots + 1, low, edge), F32),
            pltpu.VMEM((slots + 1, low, edge), F32),
            pltpu.VMEM((max(rb, CB_DEV), 2 * edge, edge), BF16),
            pltpu.VMEM((max(rb, CB_DEV), 2 * edge, edge), BF16),
            pltpu.VMEM((2, 2, rb, low, edge), BF16),
            pltpu.VMEM((2, 2, 2 * hp, edge), F32),
            pltpu.VMEM((2, 2, hp, edge), F32),
            pltpu.VMEM((2, 2, nz, sr, edge), BF16),
            pltpu.VMEM((2, 2, nz, sr, edge), BF16),
            pltpu.VMEM((2, 2, 2 * hp, edge), BF16),
            pltpu.VMEM((2, 2, rb, low, edge), BF16),
            pltpu.VMEM((2, 2, nf, own, low, edge), BF16),
            pltpu.VMEM((2, own * low, edge), F32),
            pltpu.VMEM((2, sr, edge), F32),
            pltpu.VMEM((2, own * low, edge), F32),
            pltpu.SMEM((2 * slots + CB_DEV + rb,), jnp.int32),
            pltpu.VMEM((2, 2, 8, edge), F32),
            pltpu.VMEM((2, 2, nf, 8, edge), F32),
            pltpu.VMEM((2, 2, 8, edge), F32),
            pltpu.VMEM((2, 2, 2 * nz, 8, edge), F32),
            pltpu.SemaphoreType.DMA((n_copies,)),
            pltpu.SemaphoreType.DMA((n_copies,)),
        ],
        compiler_params=pltpu.CompilerParams(
            collective_id=0, has_side_effects=True, vmem_limit_bytes=48 * 1024 * 1024
        ),
        cost_estimate=pl.CostEstimate(
            flops=8 * slots * edge**3, bytes_accessed=4 * 1024 * 1024, transcendentals=0
        ),
    )(rows, cols, count, values, right_side, penalties)


def solution(mesh):
    nz, nf = mesh.shape["comp"] // 2, mesh.shape["feat"]
    placed = (
        P("comp", "feat", None, None, None),
        P("comp", "feat", None),
        P("comp", "feat", None),
        P("comp", "feat"),
        P(("comp", "feat"), None),
        P(),
    )
    return jax.shard_map(
        functools.partial(shards, nz, nf),
        mesh=mesh,
        in_specs=placed,
        out_specs=(P("feat", None), P(("comp", "feat"), None)),
        check_vma=False,
    )
```

time: 90.7 us -> 84.8 us (0.935)
  Pallas kernels: 84.8 us -> 78.1 us
    pallas_call x1, Pallas kernels: 84.8 us -> 78.1 us  [shards(): pl.pallas_call(functools.partial(kernel, nz, nf, slots, rb, edge, sr), ou...]
where the time goes in v2:
time: 84.8 us; the launch traced here: 84.6 us
  Pallas kernels  78.1 us (92%)
  local copies, waits for them, and re-layouts  5.11 us (6%)
  between operations  1.3 us (2%)
    pallas_call x1, Pallas kernels, shards(): pl.pallas_call(functools.partial(kernel, nz, nf, slots, rb, edge, sr), ou...  78.1 us
    unnamed x12, local copies, waits for them, and re-layouts  4.95 us

profile of v2, /device:TPU:0, one launch (start us, length us, event | category | flops | bytes accessed | tf_op | source)
XLA Modules:
  0.0 84.6 jit_solution(7827345021719124372)
XLA Ops:
  1.3 0.0 copy-start.4
  1.3 0.6 copy-done.4
  1.9 0.1 tile.10
  2.0 0.0 copy-start.2
  2.0 0.0 copy-start.3
  2.0 0.1 tile.12.ridge
  2.1 0.6 copy-done.2
  2.7 0.0 copy-done.3
  2.7 0.0 copy-start
  2.7 1.1 %copy-done = bf16[1,1,24,128,128]{4,3,2,1,0:T(8,128)(2,1)S(1)} copy-done((bf16[1,1,24,128,128]{4,3,2,1,0:T(8,128)(2,1)S(1)}, bf16[1,1,24,128,128]{4,3,2,1,0:T(8,128)(2,1)}, u32[]{:S(2)}) %copy-start) | copy-done | bytes 786456
  3.8 0.0 copy-start.1
  3.8 0.9 %copy-done.1 = f32[512,128]{1,0:T(8,128)S(1)} copy-done((f32[512,128]{1,0:T(8,128)S(1)}, f32[512,128]{1,0:T(8,128)}, u32[]{:S(2)}) %copy-start.1) | copy-done | bytes 262168
  4.8 78.1 %shard_map.77 = (f32[1792,128]{1,0:T(8,128)S(1)}, f32[512,128]{1,0:T(8,128)S(1)}) custom-call(s32[24]{0:T(128)S(1)} %bitcast.6, s32[24]{0:T(128)S(1)} %bitcast.7, s32[1]{0:T(128)} %bitcast.4.count, bf16[24,128,128]{2,1,0:T(8,128)(2,1)S(1)} %bitcast.5, f32[512,128]{1,0:T(8,128)S(1)} %copy-done.1, f32[2,128]{1,0:T(2,128)S(1)} %tile.12.ridge), custom_call_target="tpu_custom_call" | custom-call | flops 402653184 | bytes 4194304 | tf_op jit(solution)/shard_map/pallas_call | solution.py:322
  82.9 0.9 %copy.11 = f32[1792,128]{1,0:T(8,128)} copy(f32[1792,128]{1,0:T(8,128)S(1)} %get-tuple-element.4) | data formatting | bytes 1835008
  83.9 0.7 copy.12
  (1 shorter events, 0.0 us)
Async XLA Ops:
  1.3 0.7 copy-start.4
  2.0 0.7 copy-start.2
  2.0 0.7 copy-start.3
  2.7 1.1 %copy-start = (bf16[1,1,24,128,128]{4,3,2,1,0:T(8,128)(2,1)S(1)}, bf16[1,1,24,128,128]{4,3,2,1,0:T(8,128)(2,1)}, u32[]{:S(2)}) copy-start(bf16[1,1,24,128,128]{4,3,2,1,0:T(8,128)(2,1)} %param.6) | copy-start | bytes 2359300
  3.8 0.9 %copy-start.1 = (f32[512,128]{1,0:T(8,128)S(1)}, f32[512,128]{1,0:T(8,128)}, u32[]{:S(2)}) copy-start(f32[512,128]{1,0:T(8,128)} %rs.1) | copy-start | bytes 786436

commit v3 on v2

--- a/solution.py
+++ b/solution.py
@@ -20,7 +20,7 @@
 def kernel(
     nz, nf, slots, rb, edge, sr,
     rows, cols, count, values, rs, ridge, sol_out, res_out,
-    vt, run_a, run_b, wide_a, wide_b, slabs, part, sib, pair, zbuf, dirs, img, rbuf,
+    vt, run_a, run_b, panel_a, panel_b, chosen_a, chosen_b, product_a, product_b, slabs, part, sib, pair, zbuf, dirs, img, rbuf,
     r_f32, g_f32, i_f32, link, sc_src, sc_feat, sc_mid, sc_comp, send_sems, recv_sems,
 ):
     comp, feat = lax.axis_index("comp"), lax.axis_index("feat")
@@ -65,36 +65,39 @@
     prev_c, last_c = 0, slots
     prev_r, last_r = slots + CB_DEV, 2 * slots + CB_DEV
 
-    def last_slot(keys, wanted, limit):
-        found = jnp.int32(slots)
-        for t in range(slots):
-            found = jnp.where((keys[t] == wanted) & (t < limit), t, found)
-        return found
-
     def make_links(keys, groups, prev, last):
-        @pl.loop(0, slots)
-        def _(s):
-            link[prev + s] = last_slot(keys, keys[s], s)
-
+        seen = [jnp.int32(slots) for _ in range(groups)]
         live = count[0]
-
-        @pl.loop(0, groups)
-        def _(q):
-            link[last + q] = last_slot(keys, q, live)
+        for s in range(slots):
+            key = keys[s]
+            before = jnp.int32(slots)
+            for q in range(groups):
+                before = jnp.where(key == q, seen[q], before)
+            link[prev + s] = before
+            key = jnp.where(s < live, key, -1)
+            for q in range(groups):
+                seen[q] = jnp.where(key == q, s, seen[q])
+        for q in range(groups):
+            link[last + q] = seen[q]
 
     left = lax.broadcasted_iota(jnp.int32, (low, edge), 1) < low
 
     def swap(x):
         return pltpu.roll(x, low, axis=1)
 
-    def widen(wide, at, packed):
+    def widen(packed):
         x = packed.astype(F32)
         y = swap(x)
         zero = jnp.zeros_like(x)
-        wide[at, pl.ds(0, low)] = jnp.where(left, x, zero).astype(BF16)
-        wide[at, pl.ds(low, low)] = jnp.where(left, y, zero).astype(BF16)
-        wide[at, pl.ds(2 * low, low)] = jnp.where(left, zero, y).astype(BF16)
-        wide[at, pl.ds(3 * low, low)] = jnp.where(left, zero, x).astype(BF16)
+        return jnp.concatenate(
+            [
+                jnp.where(left, x, zero).astype(BF16),
+                jnp.where(left, y, zero).astype(BF16),
+                jnp.where(left, zero, y).astype(BF16),
+                jnp.where(left, zero, x).astype(BF16),
+            ],
+            axis=0,
+        )
 
     def unpack(x0, x1):
         return jnp.where(left, x0, swap(x1)), jnp.where(left, swap(x0), x1)
@@ -104,7 +107,9 @@
 
     def stream(h):
         run = (run_a, run_b)[h]
-        wide = (wide_a, wide_b)[h]
+        panel = (panel_a, panel_b)[h]
+        chosen = (chosen_a, chosen_b)[h]
+        product = (product_a, product_b)[h]
 
         def gather_feat(it):
             at = (it, h, mine)
@@ -112,13 +117,16 @@
 
         def products(blocks, places, prev):
             for s in range(slots):
+                chosen[s] = panel[places[s]]
+            for s in range(slots):
                 block = jnp.concatenate([blocks[s, :low], blocks[s, low:]], axis=1)
-                product = jnp.dot(block, wide[places[s]], preferred_element_type=F32)
-                run[s] = product + run[link[prev + s]]
+                product[s] = jnp.dot(block, widen(chosen[s]), preferred_element_type=F32)
+            for s in range(slots):
+                run[s] = product[s] + run[link[prev + s]]
 
         def backward(it):
             for r in range(rb):
-                widen(wide, r, slabs[it, h, r])
+                panel[r] = slabs[it, h, r]
             products(vt, rows, prev_c)
             for q in range(CB_DEV):
                 d, p = q // (CB_DEV // 2), q % (CB_DEV // 2)
@@ -170,7 +178,7 @@
         def forward(it):
             for q in range(CB_DEV):
                 d, p = q // (CB_DEV // 2), q % (CB_DEV // 2)
-                widen(wide, q, dirs[it, h, pl.ds(d * hp + p * low, low)])
+                panel[q] = dirs[it, h, pl.ds(d * hp + p * low, low)]
             products(values, cols, prev_r)
             for r in range(rb):
                 img[it, h, r] = run[link[last_r + r]].astype(BF16)
@@ -331,8 +339,12 @@
             pltpu.VMEM((slots, edge, edge), BF16),
             pltpu.VMEM((slots + 1, low, edge), F32),
             pltpu.VMEM((slots + 1, low, edge), F32),
-            pltpu.VMEM((max(rb, CB_DEV), 2 * edge, edge), BF16),
-            pltpu.VMEM((max(rb, CB_DEV), 2 * edge, edge), BF16),
+            pltpu.VMEM((max(rb, CB_DEV), low, edge), BF16),
+            pltpu.VMEM((max(rb, CB_DEV), low, edge), BF16),
+            pltpu.VMEM((slots, low, edge), BF16),
+            pltpu.VMEM((slots, low, edge), BF16),
+            pltpu.VMEM((slots, low, edge), F32),
+            pltpu.VMEM((slots, low, edge), F32),
             pltpu.VMEM((2, 2, rb, low, edge), BF16),
             pltpu.VMEM((2, 2, 2 * hp, edge), F32),
             pltpu.VMEM((2, 2, hp, edge), F32),

time: 84.8 us -> 84.5 us (level)
  no operation moved by 1% of the time
where the time goes in v3:
time: 84.5 us; the launch traced here: 84.3 us
  Pallas kernels  77.9 us (92%)
  local copies, waits for them, and re-layouts  5.11 us (6%)
  between operations  1.3 us (2%)
    pallas_call x1, Pallas kernels, shards(): pl.pallas_call(functools.partial(kernel, nz, nf, slots, rb, edge, sr), ou...  77.9 us
    unnamed x12, local copies, waits for them, and re-layouts  4.95 us

profile of v3, /device:TPU:0, one launch (start us, length us, event | category | flops | bytes accessed | tf_op | source)
XLA Modules:
  0.0 84.3 jit_solution(12462016878484578502)
XLA Ops:
  1.3 0.0 copy-start.4
  1.3 0.6 copy-done.4
  1.9 0.1 tile.10
  2.0 0.0 copy-start.2
  2.0 0.0 copy-start.3
  2.0 0.1 tile.12.ridge
  2.1 0.6 copy-done.2
  2.7 0.0 copy-done.3
  2.7 0.0 copy-start
  2.7 1.1 %copy-done = bf16[1,1,24,128,128]{4,3,2,1,0:T(8,128)(2,1)S(1)} copy-done((bf16[1,1,24,128,128]{4,3,2,1,0:T(8,128)(2,1)S(1)}, bf16[1,1,24,128,128]{4,3,2,1,0:T(8,128)(2,1)}, u32[]{:S(2)}) %copy-start) | copy-done | bytes 786456
  3.8 0.0 copy-start.1
  3.8 0.9 %copy-done.1 = f32[512,128]{1,0:T(8,128)S(1)} copy-done((f32[512,128]{1,0:T(8,128)S(1)}, f32[512,128]{1,0:T(8,128)}, u32[]{:S(2)}) %copy-start.1) | copy-done | bytes 262168
  4.8 77.9 %shard_map.77 = (f32[1792,128]{1,0:T(8,128)S(1)}, f32[512,128]{1,0:T(8,128)S(1)}) custom-call(s32[24]{0:T(128)S(1)} %bitcast.6, s32[24]{0:T(128)S(1)} %bitcast.7, s32[1]{0:T(128)} %bitcast.4.count, bf16[24,128,128]{2,1,0:T(8,128)(2,1)S(1)} %bitcast.5, f32[512,128]{1,0:T(8,128)S(1)} %copy-done.1, f32[2,128]{1,0:T(2,128)S(1)} %tile.12.ridge), custom_call_target="tpu_custom_call" | custom-call | flops 402653184 | bytes 4194304 | tf_op jit(solution)/shard_map/pallas_call | solution.py:330
  82.7 0.9 %copy.11 = f32[1792,128]{1,0:T(8,128)} copy(f32[1792,128]{1,0:T(8,128)S(1)} %get-tuple-element.4) | data formatting | bytes 1835008
  83.6 0.7 copy.12
  (1 shorter events, 0.0 us)
Async XLA Ops:
  1.3 0.7 copy-start.4
  2.0 0.7 copy-start.2
  2.0 0.7 copy-start.3
  2.7 1.1 %copy-start = (bf16[1,1,24,128,128]{4,3,2,1,0:T(8,128)(2,1)S(1)}, bf16[1,1,24,128,128]{4,3,2,1,0:T(8,128)(2,1)}, u32[]{:S(2)}) copy-start(bf16[1,1,24,128,128]{4,3,2,1,0:T(8,128)(2,1)} %param.6) | copy-start | bytes 2359300
  3.8 0.9 %copy-start.1 = (f32[512,128]{1,0:T(8,128)S(1)}, f32[512,128]{1,0:T(8,128)}, u32[]{:S(2)}) copy-start(f32[512,128]{1,0:T(8,128)} %rs.1) | copy-start | bytes 786436

commit v4 on v3

--- a/solution.py
+++ b/solution.py
@@ -281,16 +281,18 @@
 
     streams = [stream(h) for h in range(2)]
     steps = [None, None]
-    for g in streams:
-        next(g)
+    next(streams[0])
     run_a[slots] = jnp.zeros((low, edge), F32)
     run_b[slots] = jnp.zeros((low, edge), F32)
     for s in range(slots):
         vt[s] = values[s].T
     make_links(cols, CB_DEV, prev_c, last_c)
     make_links(rows, rb, prev_r, last_r)
+    next(streams[0])
     while None in steps:
-        for h, g in enumerate(streams):
+        for h, g in reversed(list(enumerate(streams))):
+            if steps[h] is not None:
+                continue
             try:
                 next(g)
             except StopIteration as done:

time: 84.5 us -> 81.7 us (0.967)
  Pallas kernels: 77.9 us -> 75.1 us
    pallas_call x1, Pallas kernels: 77.9 us -> 75.1 us  [shards(): pl.pallas_call(functools.partial(kernel, nz, nf, slots, rb, edge, sr), ou...]
where the time goes in v4:
time: 81.7 us; the launch traced here: 81.5 us
  Pallas kernels  75.1 us (92%)
  local copies, waits for them, and re-layouts  5.11 us (6%)
  between operations  1.3 us (2%)
    pallas_call x1, Pallas kernels, shards(): pl.pallas_call(functools.partial(kernel, nz, nf, slots, rb, edge, sr), ou...  75.1 us
    unnamed x12, local copies, waits for them, and re-layouts  4.95 us

profile of v4, /device:TPU:0, one launch (start us, length us, event | category | flops | bytes accessed | tf_op | source)
XLA Modules:
  0.0 81.5 jit_solution(8672401631441467780)
XLA Ops:
  1.3 0.0 copy-start.4
  1.3 0.6 copy-done.4
  1.9 0.1 tile.10
  2.0 0.0 copy-start.2
  2.0 0.0 copy-start.3
  2.0 0.1 tile.12.ridge
  2.1 0.6 copy-done.2
  2.7 0.0 copy-done.3
  2.7 0.0 copy-start
  2.7 1.1 %copy-done = bf16[1,1,24,128,128]{4,3,2,1,0:T(8,128)(2,1)S(1)} copy-done((bf16[1,1,24,128,128]{4,3,2,1,0:T(8,128)(2,1)S(1)}, bf16[1,1,24,128,128]{4,3,2,1,0:T(8,128)(2,1)}, u32[]{:S(2)}) %copy-start) | copy-done | bytes 786456
  3.8 0.0 copy-start.1
  3.8 0.9 %copy-done.1 = f32[512,128]{1,0:T(8,128)S(1)} copy-done((f32[512,128]{1,0:T(8,128)S(1)}, f32[512,128]{1,0:T(8,128)}, u32[]{:S(2)}) %copy-start.1) | copy-done | bytes 262168
  4.8 75.1 %shard_map.77 = (f32[1792,128]{1,0:T(8,128)S(1)}, f32[512,128]{1,0:T(8,128)S(1)}) custom-call(s32[24]{0:T(128)S(1)} %bitcast.6, s32[24]{0:T(128)S(1)} %bitcast.7, s32[1]{0:T(128)} %bitcast.4.count, bf16[24,128,128]{2,1,0:T(8,128)(2,1)S(1)} %bitcast.5, f32[512,128]{1,0:T(8,128)S(1)} %copy-done.1, f32[2,128]{1,0:T(2,128)S(1)} %tile.12.ridge), custom_call_target="tpu_custom_call" | custom-call | flops 402653184 | bytes 4194304 | tf_op jit(solution)/shard_map/pallas_call | solution.py:332
  79.9 0.9 %copy.11 = f32[1792,128]{1,0:T(8,128)} copy(f32[1792,128]{1,0:T(8,128)S(1)} %get-tuple-element.4) | data formatting | bytes 1835008
  80.8 0.7 copy.12
  (1 shorter events, 0.0 us)
Async XLA Ops:
  1.3 0.7 copy-start.4
  2.0 0.7 copy-start.2
  2.0 0.7 copy-start.3
  2.7 1.1 %copy-start = (bf16[1,1,24,128,128]{4,3,2,1,0:T(8,128)(2,1)S(1)}, bf16[1,1,24,128,128]{4,3,2,1,0:T(8,128)(2,1)}, u32[]{:S(2)}) copy-start(bf16[1,1,24,128,128]{4,3,2,1,0:T(8,128)(2,1)} %param.6) | copy-start | bytes 2359300
  3.8 0.9 %copy-start.1 = (f32[512,128]{1,0:T(8,128)S(1)}, f32[512,128]{1,0:T(8,128)}, u32[]{:S(2)}) copy-start(f32[512,128]{1,0:T(8,128)} %rs.1) | copy-start | bytes 786436

commit v5 on v4

--- a/solution.py
+++ b/solution.py
@@ -19,9 +19,9 @@
 
 def kernel(
     nz, nf, slots, rb, edge, sr,
-    rows, cols, count, values, rs, ridge, sol_out, res_out,
-    vt, run_a, run_b, panel_a, panel_b, chosen_a, chosen_b, product_a, product_b, slabs, part, sib, pair, zbuf, dirs, img, rbuf,
-    r_f32, g_f32, i_f32, link, sc_src, sc_feat, sc_mid, sc_comp, send_sems, recv_sems,
+    rows, cols, count, values_in, rs_in, ridge, sol_out, res_out,
+    values, rs, vt, run_a, run_b, panel_a, panel_b, chosen_a, chosen_b, product_a, product_b, slabs, part, sib, pair, zbuf, dirs, img, rbuf,
+    r_f32, g_f32, i_f32, link, sc_src, sc_feat, sc_mid, sc_comp, load_sems, send_sems, recv_sems,
 ):
     comp, feat = lax.axis_index("comp"), lax.axis_index("feat")
     core, z = lax.rem(comp, 2), comp // 2
@@ -137,17 +137,13 @@
 
         def scatter_comp(it):
             order = list(range(1, nz)) + [0]
-            halves = {}
-            for k in order:
-                theirs = pl.multiple_of((1 - core) * hp + shard(k), 16)
-                halves[k] = send(
-                    part.at[it, h, pl.ds(theirs, sr)], sib.at[it, h, pl.ds(shard(k), sr)], sibling
-                )
+            theirs = pl.multiple_of((1 - core) * hp, 16)
+            whole = send(part.at[it, h, pl.ds(theirs, hp)], sib.at[it, h], sibling)
             yield
             arrivals = []
             total = None
+            whole.wait_recv()
             for k in order:
-                halves[k].wait_recv()
                 ours = pl.multiple_of(core * hp + shard(k), 16)
                 both = part[it, h, pl.ds(ours, sr)] + sib[it, h, pl.ds(shard(k), sr)]
                 if k:
@@ -165,15 +161,13 @@
             here = (it, h, pl.ds(pl.multiple_of(core * hp + shard(0), 16), sr))
             dirs[here] = piece.astype(BF16)
             across = [send(dirs.at[here], dirs.at[here], zpeer(k)) for k in range(1, nz)]
-            beside = [send(dirs.at[here], dirs.at[here], sibling)]
-            yield
-            for k, copy in zip(range(1, nz), across):
+            yield
+            for copy in across:
                 copy.wait_recv()
-                came = (it, h, pl.ds(pl.multiple_of(core * hp + shard(nz - k), 16), sr))
-                beside.append(send(dirs.at[came], dirs.at[came], sibling))
-            yield
-            for copy in beside:
-                copy.wait_recv()
+            ours = (it, h, pl.ds(pl.multiple_of(core * hp, 16), hp))
+            beside = send(dirs.at[ours], dirs.at[ours], sibling)
+            yield
+            beside.wait_recv()
 
         def forward(it):
             for q in range(CB_DEV):
@@ -265,18 +259,23 @@
         r_f32[h] = r_f32[h] - weight * i_f32[h] - step1 * u
         return weight, step1
 
+    load_rs = pltpu.make_async_copy(rs_in, rs, load_sems.at[0])
+    load_rs.start()
+    load_values = pltpu.make_async_copy(values_in, values, load_sems.at[1])
+    load_values.start()
     barrier = pltpu.get_barrier_semaphore()
     for k in range(1, n_comp):
         pl.semaphore_signal(barrier, inc=1, device_id=cpeer(k), device_id_type=MESH)
     for k in range(1, nf):
         pl.semaphore_signal(barrier, inc=1, device_id=fpeer(k), device_id_type=MESH)
+    sc_src[...] = jnp.zeros_like(sc_src)
+    load_rs.wait()
     for r in range(own_blocks):
         top, bottom = rs[pl.ds(r * edge, low)], rs[pl.ds(r * edge + low, low)]
         for h, x in enumerate(unpack(top, bottom)):
             r_f32[h, pl.ds(r * low, low)] = x
     for h in range(2):
         slabs[0, h, mine] = r_f32[h].astype(BF16).reshape(own_blocks, low, edge)
-    sc_src[...] = jnp.zeros_like(sc_src)
     pl.semaphore_wait(barrier, n_comp - 1 + nf - 1)
 
     streams = [stream(h) for h in range(2)]
@@ -284,15 +283,21 @@
     next(streams[0])
     run_a[slots] = jnp.zeros((low, edge), F32)
     run_b[slots] = jnp.zeros((low, edge), F32)
+    make_links(cols, CB_DEV, prev_c, last_c)
+    make_links(rows, rb, prev_r, last_r)
+    load_values.wait()
     for s in range(slots):
         vt[s] = values[s].T
-    make_links(cols, CB_DEV, prev_c, last_c)
-    make_links(rows, rb, prev_r, last_r)
     next(streams[0])
+    turns, done_sends = [0], 0
     while None in steps:
         for h, g in reversed(list(enumerate(streams))):
             if steps[h] is not None:
                 continue
+            turns.append(len(pending))
+            while done_sends < turns[max(len(turns) - 4, 0)]:
+                pending[done_sends].wait_send()
+                done_sends += 1
             try:
                 next(g)
             except StopIteration as done:
@@ -311,7 +316,7 @@
         parts = unpack(*found)
         for d in range(2):
             sol_out[pl.ds(q * edge + d * low, low)] = parts[d]
-    for copy in pending:
+    for copy in pending[done_sends:]:
         copy.wait_send()
 
 
@@ -325,9 +330,10 @@
     sr = -(-(CB_DEV // 2 * low) // (nz * 16)) * 16
     hp = nz * sr
     own = rb // nf
-    n_copies = 4 * (2 * (nf - 1) + 2 * (nz - 1) + 2 * nz + (nf - 1) + (2 * nz - 1))
+    n_copies = 4 * (2 * (nf - 1) + 2 * (nz - 1) + 2 + (nf - 1) + (2 * nz - 1))
     penalties = jnp.tile(ridge.reshape(2, low), (1, 2))
     smem = pl.BlockSpec(memory_space=pltpu.SMEM)
+    anywhere = pl.BlockSpec(memory_space=pl.ANY)
     vmem = pl.BlockSpec(memory_space=pltpu.VMEM)
     return pl.pallas_call(
         functools.partial(kernel, nz, nf, slots, rb, edge, sr),
@@ -335,9 +341,11 @@
             jax.ShapeDtypeStruct((CB_DEV * edge, edge), F32),
             jax.ShapeDtypeStruct((held, edge), F32),
         ),
-        in_specs=[smem, smem, smem, vmem, vmem, vmem],
+        in_specs=[smem, smem, smem, anywhere, anywhere, vmem],
         out_specs=(vmem, vmem),
         scratch_shapes=[
+            pltpu.VMEM((slots, edge, edge), BF16),
+            pltpu.VMEM((held, edge), F32),
             pltpu.VMEM((slots, edge, edge), BF16),
             pltpu.VMEM((slots + 1, low, edge), F32),
             pltpu.VMEM((slots + 1, low, edge), F32),
@@ -363,11 +371,12 @@
             pltpu.VMEM((2, 2, nf, 8, edge), F32),
             pltpu.VMEM((2, 2, 8, edge), F32),
             pltpu.VMEM((2, 2, 2 * nz, 8, edge), F32),
+            pltpu.SemaphoreType.DMA((2,)),
             pltpu.SemaphoreType.DMA((n_copies,)),
             pltpu.SemaphoreType.DMA((n_copies,)),
         ],
         compiler_params=pltpu.CompilerParams(
-            collective_id=0, has_side_effects=True, vmem_limit_bytes=48 * 1024 * 1024
+            collective_id=0, has_side_effects=True, vmem_limit_bytes=56 * 1024 * 1024
         ),
         cost_estimate=pl.CostEstimate(
             flops=8 * slots * edge**3, bytes_accessed=4 * 1024 * 1024, transcendentals=0

time: 81.7 us -> 81.9 us (level)
  Pallas kernels: 75.1 us -> 76.1 us
  local copies, waits for them, and re-layouts: 5.11 us -> 4.29 us
    unnamed x12 -> x6, local copies, waits for them, and re-layouts: 4.95 us -> 3.56 us
    pallas_call x1, Pallas kernels: 75.1 us -> 76.1 us  [shards(): pl.pallas_call(functools.partial(kernel, nz, nf, slots, rb, edge, sr), ou...]
where the time goes in v5:
time: 81.9 us; the launch traced here: 81.7 us
  Pallas kernels  76.1 us (93%)
  local copies, waits for them, and re-layouts  4.29 us (5%)
  between operations  1.3 us (2%)
    pallas_call x1, Pallas kernels, shards(): pl.pallas_call(functools.partial(kernel, nz, nf, slots, rb, edge, sr), ou...  76.1 us
    unnamed x6, local copies, waits for them, and re-layouts  3.56 us

profile of v5, /device:TPU:0, one launch (start us, length us, event | category | flops | bytes accessed | tf_op | source)
XLA Modules:
  0.0 81.7 jit_solution(10708309487947359789)
XLA Ops:
  1.3 0.0 copy-start.1
  1.3 0.6 copy-done.1
  1.9 0.1 tile.10
  2.0 0.6 tile.12.ridge
  2.7 76.1 %shard_map.77 = (f32[1792,128]{1,0:T(8,128)}, f32[512,128]{1,0:T(8,128)}) custom-call(s32[24]{0:T(128)} %bitcast.6, s32[24]{0:T(128)} %bitcast.7, s32[1]{0:T(128)} %bitcast.4.count, bf16[24,128,128]{2,1,0:T(8,128)(2,1)} %bitcast.5, f32[512,128]{1,0:T(8,128)} %rs_in.1, f32[2,128]{1,0:T(2,128)} %tile.12.ridge), custom_call_target="tpu_custom_call" | custom-call | flops 402653184 | bytes 4194304 | tf_op jit(solution)/shard_map/pallas_call | solution.py:338
  78.8 0.0 copy-start
  78.8 2.2 %copy.11 = f32[1792,128]{1,0:T(8,128)} copy(f32[1792,128]{1,0:T(8,128)} %get-tuple-element.4) | data formatting | bytes 1835008
  81.0 0.0 copy-done
  81.0 0.7 copy.12
  (1 shorter events, 0.0 us)
Async XLA Ops:
  1.3 0.7 copy-start.1
  78.8 2.2 %copy-start = (f32[512,128]{1,0:T(8,128)S(1)}, f32[512,128]{1,0:T(8,128)}, u32[]{:S(2)}) copy-start(f32[512,128]{1,0:T(8,128)} %get-tuple-element.5) | copy-start | bytes 786436

commit v6 on v5

--- a/solution.py
+++ b/solution.py
@@ -227,7 +227,9 @@
         i_f32[h] = i0
         g0 = g_f32[h]
         first = yield from sums(0, [column_sum(i0 * i0), column_sum(g0 * g0)])
-        penalty = ridge[pl.ds(h, 1)]
+        every = jnp.broadcast_to(ridge[...], (8, edge))
+        here, there = (every, swap(every)) if h == 0 else (swap(every), every)
+        penalty = jnp.where(left[:8], here, there)[0:1]
         image0, energy0 = first[0:1], first[1:2]
         step0 = energy0 / (image0 + penalty * energy0)
         r1 = r_f32[h] - step0 * i_f32[h]
@@ -331,9 +333,8 @@
     hp = nz * sr
     own = rb // nf
     n_copies = 4 * (2 * (nf - 1) + 2 * (nz - 1) + 2 + (nf - 1) + (2 * nz - 1))
-    penalties = jnp.tile(ridge.reshape(2, low), (1, 2))
     smem = pl.BlockSpec(memory_space=pltpu.SMEM)
-    anywhere = pl.BlockSpec(memory_space=pl.ANY)
+    anywhere = pl.BlockSpec(memory_space=pltpu.HBM)
     vmem = pl.BlockSpec(memory_space=pltpu.VMEM)
     return pl.pallas_call(
         functools.partial(kernel, nz, nf, slots, rb, edge, sr),
@@ -376,12 +377,12 @@
             pltpu.SemaphoreType.DMA((n_copies,)),
         ],
         compiler_params=pltpu.CompilerParams(
-            collective_id=0, has_side_effects=True, vmem_limit_bytes=56 * 1024 * 1024
+            collective_id=0, has_side_effects=True, vmem_limit_bytes=48 * 1024 * 1024
         ),
         cost_estimate=pl.CostEstimate(
             flops=8 * slots * edge**3, bytes_accessed=4 * 1024 * 1024, transcendentals=0
         ),
-    )(rows, cols, count, values, right_side, penalties)
+    )(rows, cols, count, values, right_side, ridge.reshape(1, edge))
 
 
 def solution(mesh):

time: 81.9 us -> 80.8 us (0.987)
  Pallas kernels: 76.1 us -> 74.9 us
    pallas_call x1, Pallas kernels: 76.1 us -> 74.9 us  [shards(): pl.pallas_call(functools.partial(kernel, nz, nf, slots, rb, edge, sr), ou...]
    unnamed x6 -> x12, local copies, waits for them, and re-layouts: 3.56 us -> 4.37 us
where the time goes in v6:
time: 80.8 us; the launch traced here: 80.6 us
  Pallas kernels  74.9 us (93%)
  local copies, waits for them, and re-layouts  4.37 us (5%)
  between operations  1.31 us (2%)
    pallas_call x1, Pallas kernels, shards(): pl.pallas_call(functools.partial(kernel, nz, nf, slots, rb, edge, sr), ou...  74.9 us
    unnamed x12, local copies, waits for them, and re-layouts  4.37 us

profile of v6, /device:TPU:0, one launch (start us, length us, event | category | flops | bytes accessed | tf_op | source)
XLA Modules:
  0.0 80.6 jit_solution(5078000404897723614)
XLA Ops:
  1.3 0.0 copy-start.2
  1.3 0.0 copy-start.3
  1.3 0.0 copy-start.4
  1.3 0.6 copy-done.2
  1.9 0.0 copy-done.3
  1.9 0.0 copy-done.4
  2.0 0.0 copy-start
  2.0 1.1 %copy-done = bf16[1,1,24,128,128]{4,3,2,1,0:T(8,128)(2,1)S(1)} copy-done((bf16[1,1,24,128,128]{4,3,2,1,0:T(8,128)(2,1)S(1)}, bf16[1,1,24,128,128]{4,3,2,1,0:T(8,128)(2,1)}, u32[]{:S(2)}) %copy-start) | copy-done | bytes 786456
  3.1 0.0 copy-start.1
  3.1 0.9 %copy-done.1 = f32[512,128]{1,0:T(8,128)S(1)} copy-done((f32[512,128]{1,0:T(8,128)S(1)}, f32[512,128]{1,0:T(8,128)}, u32[]{:S(2)}) %copy-start.1) | copy-done | bytes 262168
  4.0 74.9 %shard_map.77 = (f32[1792,128]{1,0:T(8,128)S(1)}, f32[512,128]{1,0:T(8,128)S(1)}) custom-call(s32[24]{0:T(128)S(1)} %bitcast.7, s32[24]{0:T(128)S(1)} %bitcast.8, s32[1]{0:T(128)} %bitcast.5.count, bf16[24,128,128]{2,1,0:T(8,128)(2,1)S(1)} %bitcast.6, f32[512,128]{1,0:T(8,128)S(1)} %copy-done.1, f32[1,128]{1,0:T(1,128)S(1)} %bitcast.9), custom_call_target="tpu_custom_call" | custom-call | flops 402653184 | bytes 4194304 | tf_op jit(solution)/shard_map/pallas_call | solution.py:339
  79.0 0.9 %copy.11 = f32[1792,128]{1,0:T(8,128)} copy(f32[1792,128]{1,0:T(8,128)S(1)} %get-tuple-element.4) | data formatting | bytes 1835008
  79.9 0.7 copy.12
Async XLA Ops:
  1.3 0.7 copy-start.2
  1.3 0.7 copy-start.3
  1.3 0.7 copy-start.4
  2.0 1.1 %copy-start = (bf16[1,1,24,128,128]{4,3,2,1,0:T(8,128)(2,1)S(1)}, bf16[1,1,24,128,128]{4,3,2,1,0:T(8,128)(2,1)}, u32[]{:S(2)}) copy-start(bf16[1,1,24,128,128]{4,3,2,1,0:T(8,128)(2,1)} %param.6) | copy-start | bytes 2359300
  3.1 0.9 %copy-start.1 = (f32[512,128]{1,0:T(8,128)S(1)}, f32[512,128]{1,0:T(8,128)}, u32[]{:S(2)}) copy-start(f32[512,128]{1,0:T(8,128)} %rs_in.1) | copy-start | bytes 786436
